TPU v7x, 32 devices: a whole 2x2x4 slice. The times are simulated.
32 devices in a mesh: groups: 2 (over x), space: 16 (over z, y, core).
Axes of the slice: x: 2, y: 2, z: 4, core: 2. Of those that a mesh axis runs over, the one named last changes fastest.
Arguments:
- snapshots: bfloat16 [256, 128, 128], P(('groups', 'space')), parts along dimension 0, may hold values from -6 to 6
- weights: bfloat16 [256, 128, 1024], P(('groups', 'space')), parts along dimension 0, may hold values from -6 to 6
- neighbours: int32 [256, 8], P(('groups', 'space')), parts along dimension 0, may hold values from 0 to 127, as said below
- time_of: int32 [256], P('groups'), parts along dimension 0, may hold values from 0 to 127, each once
Outputs:
- new_weights: float32 [256, 128, 1024], P(('groups', 'space')), parts along dimension 0
- cell_error: float32 [256, 128], P(('groups', 'space')), parts along dimension 0
There are 2 independent parts, one for each index of `groups`. A program takes and returns all parts, laid end to end along the dimension named above; each array names one. Nothing has to cross between parts.
Inputs may be any that keep to these rules, and one draw needn't show every extreme that they name: `neighbours`: row g lists 8 groups in a drawn order: g itself, g - 4, g + 4, and 5 more within 4 groups of g, all counted cyclically modulo 128; entries may repeat. `time_of`: each time index appears once.
All inputs are finite; a program needn't handle non-finite values.
Results may differ from a plain program's by a relative error of at most 0.002.
Values may be sent and summed in bfloat16 or wider, within the bound.
A program may use at most 64 MiB of HBM per device.

v0:
```python
import jax
import jax.numpy as jnp
from jax import lax
from jax.sharding import PartitionSpec as P

HALO = 4


def extended(x, sides, width):
    for axis, dim in sides:
        size, length = (lax.axis_size(axis), x.shape[dim])
        up = [(i, (i + 1) % size) for i in range(size)]
        down = [(j, i) for i, j in up]
        last = lax.slice_in_dim(x, length - width, length, axis=dim)
        initial = lax.slice_in_dim(x, 0, width, axis=dim)
        before = lax.ppermute(last, axis, up)
        after = lax.ppermute(initial, axis, down)
        x = jnp.concatenate([before, x, after], axis=dim)
    return x


def shards(snapshots, weights, neighbours, time_of):
    step_rate = 100.0
    g_dev = weights.shape[0]
    width = weights.shape[1]
    span = weights.shape[2]
    n_dev = lax.axis_size("space")
    total = time_of.shape[0]
    owned = lax.all_to_all(snapshots, "space", split_axis=1, concat_axis=0, tiled=True)
    padded = extended(owned, (("space", 1),), HALO)
    order = jnp.argsort(time_of)
    ordered = padded[order]
    target = jnp.roll(ordered[:, HALO : HALO + g_dev], -1, 0)
    first = lax.axis_index("space") * g_dev
    all_groups = g_dev * n_dev
    here = jnp.arange(g_dev, dtype=jnp.int32)
    local = (neighbours - (first + here)[:, None] + HALO) % all_groups + here[:, None]
    scale = 1.0 / jnp.sqrt(jnp.float32(span))
    rows_step = min(total, 256)
    turns = total // rows_step

    def block_rows(turn):
        rows = lax.dynamic_slice_in_dim(ordered, turn * rows_step, rows_step, 0)
        goal = lax.dynamic_slice_in_dim(target, turn * rows_step, rows_step, 0).astype(jnp.float32)
        inputs = rows[:, local].reshape(rows_step, g_dev, span)
        live = (turn * rows_step + jnp.arange(rows_step) < total - 1).astype(jnp.float32)[
            :, None, None
        ]
        return (inputs, goal, live)

    def add_grad(turn, grad):
        inputs, goal, live = block_rows(turn)
        pred = (
            jnp.einsum("tgc,goc->tgo", inputs, weights, preferred_element_type=jnp.float32) * scale
        )
        resid = ((pred - goal) * live).astype(jnp.bfloat16)
        return grad + jnp.einsum("tgo,tgc->goc", resid, inputs, preferred_element_type=jnp.float32)

    grad = lax.fori_loop(0, turns, add_grad, jnp.zeros((g_dev, width, span), jnp.float32))
    new_weights = weights.astype(jnp.float32) - step_rate * (grad * (2.0 * scale / (total - 1)))
    new_rounded = new_weights.astype(jnp.bfloat16)

    def add_error(turn, error):
        inputs, goal, live = block_rows(turn)
        after = (
            jnp.einsum("tgc,goc->tgo", inputs, new_rounded, preferred_element_type=jnp.float32)
            * scale
            - goal
        ) * live
        return error + jnp.sum(after * after, axis=0)

    error = lax.fori_loop(0, turns, add_error, jnp.zeros((g_dev, width), jnp.float32))
    return (new_weights, error / (total - 1))


def solution(mesh):
    return jax.shard_map(
        shards,
        mesh=mesh,
        in_specs=(
            P(("groups", "space"), None, None),
            P(("groups", "space"), None, None),
            P(("groups", "space"), None),
            P("groups"),
        ),
        out_specs=(P(("groups", "space"), None, None), P(("groups", "space"), None)),
        check_vma=False,
    )
```

profile of v0, /device:TPU:0, one launch (start us, length us, event | category | flops | bytes accessed | tf_op | source)
XLA Modules:
  0.0 38.4 jit_solution(6387515284216943299)
XLA Ops:
  0.6 1.8 %copy.21 = bf16[8,128,128]{2,0,1:T(8,128)(2,1)} copy(bf16[8,128,128]{2,1,0:T(8,128)(2,1)} %param.4) | data formatting | bytes 524288 | tf_op args[0]
  2.5 7.4 %all-to-all-start = ((bf16[8,128,128]{2,0,1:T(8,128)(2,1)}), bf16[8,128,128]{2,0,1:T(8,128)(2,1)S(1)}, u32[]{:S(2)}, u32[]{:S(2)}) async-start(bf16[8,128,128]{2,0,1:T(8,128)(2,1)} %copy.21), calls=%async_computation | async-start | bytes 524288 | tf_op jit(solution)/shard_map/all_to_all | solution.py:29
  9.9 3.2 %sort.17 = (s32[128]{0:T(128)}, s32[128]{0:T(128)S(1)}) sort(s32[128]{0:T(128)} %param.7, s32[128]{0:T(128)S(1)} %iota.22), dimensions={0}, to_apply=%region_0.0 | sort | flops 896 | bytes 2048 | tf_op jit(solution)/shard_map/jit(argsort)/sort | solution.py:31
  13.1 0.8 %compare_select_fusion = s32[8,8]{1,0:T(8,128)S(1)} fusion(s32[8,8]{1,0:T(8,128)} %param.6, s32[8]{0:T(128)S(1)} %iota_add_fusion), kind=kLoop, calls=%fused_computation.28 | loop fusion | flops 1088 | bytes 544 | tf_op jit(solution)/shard_map/while/body/eval_jaxpr/select_n | solution.py:45
  13.8 6.1 %all-to-all-done = bf16[8,128,128]{2,0,1:T(8,128)(2,1)S(1)} async-done(((bf16[8,128,128]{2,0,1:T(8,128)(2,1)}), bf16[8,128,128]{2,0,1:T(8,128)(2,1)S(1)}, u32[]{:S(2)}, u32[]{:S(2)}) %all-to-all-start) | async-done | bytes 262176 | tf_op jit(solution)/shard_map/all_to_all | solution.py:29
  19.9 0.1 fusion.63
  20.0 0.1 collective-permute-start
  20.1 4.4 %collective-permute-start.1 = (bf16[128,4,128]{2,1,0:T(4,128)(2,1)S(1)}, bf16[128,4,128]{2,1,0:T(4,128)(2,1)S(1)}, u32[]{:S(2)}, u32[]{:S(2)}) collective-permute-start(bf16[128,4,128]{2,1,0:T(4,128)(2,1)S(1)} %get-tuple-element.33), channel_id=1, source_target_pairs={{1,0},{2,1},{3,2},{4,3},{5,4},{6,5},{7,6},{8,7},{9,8},{10,9},{11,1... | collective-permute-start | bytes 393224 | tf_op jit(solution)/shard_map/ppermute | solution.py:17
  24.5 0.1 reshape.30
  24.6 2.6 %collective-permute-done = bf16[128,4,128]{2,1,0:T(4,128)(2,1)S(1)} collective-permute-done((bf16[128,4,128]{2,1,0:T(4,128)(2,1)S(1)}, bf16[128,4,128]{2,1,0:T(4,128)(2,1)S(1)}, u32[]{:S(2)}, u32[]{:S(2)}) %collective-permute-start) | collective-permute-done | bytes 131104 | tf_op jit(solution)/shard_map/ppermute | solution.py:16
  27.2 0.0 collective-permute-done.1
  27.2 0.3 pad_maximum_fusion
  27.5 0.7 %gather_fusion = bf16[128,16,128]{2,1,0:T(8,128)(2,1)S(1)} fusion(bf16[128,16,128]{2,1,0:T(8,128)(2,1)S(1)} %pad_maximum_fusion, s32[1024]{0:T(1024)S(1)} %pad_clamp_fusion.1), kind=kCustom, calls=%fused_computation | custom fusion | bytes 1049088 | tf_op jit(solution)/shard_map/gather | solution.py:32
  28.2 0.1 copy.24
  28.4 0.1 slice.27
  28.4 1.0 %gather_fusion.1 = bf16[64,128,128]{2,1,0:T(8,128)(2,1)S(1)} fusion(bf16[128,16,128]{2,0,1:T(8,128)(2,1)S(1)} %copy.24, s32[1024]{0:T(1024)S(1)} %pad_clamp_fusion), kind=kCustom, calls=%fused_computation.1 | custom fusion | bytes 4194560 | tf_op jit(solution)/shard_map/while/body/eval_jaxpr/gather | solution.py:45
  29.4 5.5 %multiply_subtract_fusion = f32[8,128,1024]{2,1,0:T(8,128)} fusion(bf16[8,128,1024]{2,1,0:T(8,128)(2,1)} %param.5, bf16[8,8,16,8,128]{4,3,2,1,0:T(8,128)(2,1)S(1)} %bitcast.60, f32[128]{0:T(128)S(1)} %compare_convert_fusion, bf16[1,8,128]{2,0,1:T(2,128)(2,1)S(1)} %slice.28, bf16[127,8,128]{2,0,1:T(8,128)(2,1)S(1)} %slice.27), kind=kOutput, calls=%fused_computation.2 | convolution fusion | flops 541065216 | bytes 8651264 | tf_op jit(solution)/shard_map/while/body/eval_jaxpr/tgo,tgc->goc/dot_general | solution.py:57
  34.9 2.9 %fusion.51 = f32[8,128]{1,0:T(8,128)S(1)} fusion(bf16[8,8,16,8,128]{4,3,2,1,0:T(8,128)(2,1)S(1)} %bitcast.61, f32[8,128,1024]{2,1,0:T(8,128)} %multiply_subtract_fusion, f32[128]{0:T(128)S(1)} %compare_convert_fusion, bf16[1,8,128]{2,0,1:T(2,128)(2,1)S(1)} %slice.28, bf16[127,8,128]{2,0,1:T(8,128)(2,1)S(1)} %slice.27), kind=kOutput, calls=%fused_computation.22 | convolution fusion | flops 270662656 | bytes 6558208 | tf_op jit(solution)/shard_map/while/body/eval_jaxpr/tgc,goc->tgo/dot_general | solution.py:66
  37.8 0.6 %broadcast_multiply_fusion = f32[8,128]{1,0:T(8,128)} fusion(f32[8,128]{1,0:T(8,128)S(1)} %fusion.51), kind=kLoop, calls=%fused_computation.37 | loop fusion | flops 1024 | bytes 8192 | tf_op jit(solution)/shard_map/div | solution.py:73
  (8 shorter events, 0.1 us)
Async XLA Ops:
  2.5 17.4 %all-to-all-start = ((bf16[8,128,128]{2,0,1:T(8,128)(2,1)}), bf16[8,128,128]{2,0,1:T(8,128)(2,1)S(1)}, u32[]{:S(2)}, u32[]{:S(2)}) async-start(bf16[8,128,128]{2,0,1:T(8,128)(2,1)} %copy.21), calls=%async_computation | async-start | bytes 524288 | tf_op jit(solution)/shard_map/all_to_all | solution.py:29
  20.0 7.1 %collective-permute-start = (bf16[128,4,128]{2,1,0:T(4,128)(2,1)S(1)}, bf16[128,4,128]{2,1,0:T(4,128)(2,1)S(1)}, u32[]{:S(2)}, u32[]{:S(2)}) collective-permute-start(bf16[128,4,128]{2,1,0:T(4,128)(2,1)S(1)} %get-tuple-element.32), channel_id=1, source_target_pairs={{0,1},{1,2},{2,3},{3,4},{4,5},{5,6},{6,7},{7,8},{8,9},{9,10},{10,1... | collective-permute-start | bytes 393224 | tf_op jit(solution)/shard_map/ppermute | solution.py:16
  20.1 7.1 %collective-permute-start.1 = (bf16[128,4,128]{2,1,0:T(4,128)(2,1)S(1)}, bf16[128,4,128]{2,1,0:T(4,128)(2,1)S(1)}, u32[]{:S(2)}, u32[]{:S(2)}) collective-permute-start(bf16[128,4,128]{2,1,0:T(4,128)(2,1)S(1)} %get-tuple-element.33), channel_id=1, source_target_pairs={{1,0},{2,1},{3,2},{4,3},{5,4},{6,5},{7,6},{8,7},{9,8},{10,9},{11,1... | collective-permute-start | bytes 393224 | tf_op jit(solution)/shard_map/ppermute | solution.py:17
where the time goes:
time: 38.7 us; the launch traced here: 38.4 us
  starting transfers between devices  11.9 us (31%)
  waiting for transfers between devices  8.62 us (22%)
  matrix products  8.4 us (22%)
  other arithmetic  4.87 us (13%)
  local copies, waits for them, and re-layouts  3.91 us (10%)
  between operations  0.72 us (2%)
    all_to_all x1, starting transfers between devices, shards(): lax.all_to_all(snapshots, 'space', split_axis=1, concat_axis=0, tiled=True)  7.39 us
    all_to_all x1, waiting for transfers between devices, shards(): lax.all_to_all(snapshots, 'space', split_axis=1, concat_axis=0, tiled=True)  6.06 us
    dot_general x1, matrix products, add_grad(): jnp.einsum('tgo,tgc->goc', resid, inputs, preferred_element_type=jnp.floa...  5.49 us
    ppermute x1, starting transfers between devices, extended(): after = lax.ppermute(initial, axis, down)  4.43 us
    sort x1, other arithmetic, shards(): order = jnp.argsort(time_of)  3.19 us
    dot_general x1, matrix products, add_error(): jnp.einsum('tgc,goc->tgo', inputs, new_rounded, preferred_element_type=jn...  2.91 us
    ppermute x1, waiting for transfers between devices, extended(): before = lax.ppermute(last, axis, up)  2.55 us
    unnamed x1, local copies, waits for them, and re-layouts  1.83 us
  transfers between devices with their start and end apart: 3, of which 2 were waited for; matrix products, arithmetic and copies ran while one was open for 11% of the time, Pallas kernels for 0%

commit v1 on v0

v1 whole, which is shorter than its diff:
```python
import functools

import jax
import jax.numpy as jnp
from jax import lax
from jax.experimental import pallas as pl
from jax.experimental.pallas import tpu as pltpu
from jax.sharding import PartitionSpec as P

HALO = 4
MESH = pl.DeviceIdType.MESH


def gather_kernel(n, snaps, x, wide, flat, recv, send_sem, recv_sem):
    rows, groups, cells = snaps.shape
    g_dev = groups // n
    span = g_dev + 2 * HALO
    me = lax.axis_index("space")

    barrier = pltpu.get_barrier_semaphore()
    for i in range(1, n):
        pl.semaphore_signal(
            barrier, inc=1, device_id={"space": lax.rem(me + i, n)}, device_id_type=MESH
        )

    step = 16

    @pl.loop(0, groups // step)
    def _(b):
        first = pl.multiple_of(b * step, step)
        block = snaps[:, pl.ds(first, step), :].astype(jnp.float32)
        wide[...] = block.reshape(rows * step, cells)
        for q in range(step // 2):
            pair = jnp.concatenate(
                [wide[pl.ds(2 * q + h, rows, stride=step), :] for h in range(2)], axis=0
            )
            at = pl.multiple_of((first + HALO + 2 * q) * rows, 2 * rows)
            flat[pl.ds(at, 2 * rows), :] = pair.astype(jnp.bfloat16)

    edge = HALO * rows
    flat[:edge, :] = flat[groups * rows : groups * rows + edge, :]
    flat[(groups + HALO) * rows :, :] = flat[edge : 2 * edge, :]

    pl.semaphore_wait(barrier, n - 1)

    def copy(i):
        to = lax.rem(me + i, n)
        part = pl.ds(pl.multiple_of(to * (g_dev * rows), g_dev * rows), span * rows)
        return pltpu.make_async_remote_copy(
            src_ref=flat.at[part, :],
            dst_ref=recv.at[me],
            send_sem=send_sem.at[i],
            recv_sem=recv_sem.at[i],
            device_id={"space": to},
            device_id_type=MESH,
        )

    order = sorted(range(1, n), key=lambda i: -min(i, n - i))
    for i in order:
        copy(i).start()

    def place(src, block):
        at = pl.multiple_of(src * rows, rows)
        x[:, pl.ds(at, rows), :] = block.reshape(span, rows, cells)

    own = pl.ds(pl.multiple_of(me * (g_dev * rows), g_dev * rows), span * rows)
    place(me, flat[own, :].astype(jnp.float32))
    for i in reversed(order):
        copy(i).wait_recv()
        src = lax.rem(me + n - i, n)
        place(src, recv[src].astype(jnp.float32))
    for i in order:
        copy(i).wait_send()


def gathered(snaps, n):
    rows, groups, cells = snaps.shape
    g_dev = groups // n
    span = g_dev + 2 * HALO
    return pl.pallas_call(
        functools.partial(gather_kernel, n),
        out_shape=jax.ShapeDtypeStruct((span, rows * n, cells), jnp.float32),
        in_specs=[pl.BlockSpec(memory_space=pltpu.VMEM)],
        out_specs=pl.BlockSpec(memory_space=pltpu.VMEM),
        scratch_shapes=[
            pltpu.VMEM((rows * 16, cells), jnp.float32),
            pltpu.VMEM(((groups + 2 * HALO) * rows, cells), jnp.bfloat16),
            pltpu.VMEM((n, span * rows, cells), jnp.bfloat16),
            pltpu.SemaphoreType.DMA((n,)),
            pltpu.SemaphoreType.DMA((n,)),
        ],
        compiler_params=pltpu.CompilerParams(
            collective_id=0, has_side_effects=True, vmem_limit_bytes=40 * 2**20
        ),
        cost_estimate=pl.CostEstimate(
            flops=0, bytes_accessed=4 * span * rows * n * cells, transcendentals=0
        ),
    )(snaps)


def step_kernel(n, per, nb, x, times, weights, fresh_out, error_out, goal, inputs, xb):
    span, total, cells = x.shape
    g_dev = span - 2 * HALO
    width = g_dev * n
    depth = weights.shape[2]
    scale = 1.0 / (depth**0.5)
    step_rate = 100.0
    me = lax.axis_index("space")
    at = pl.program_id(0)
    tile = 128
    turns = total // tile

    def columns(b):
        row = times[:, pl.ds(pl.multiple_of(b * tile, tile), tile)]
        return jnp.transpose(jnp.broadcast_to(row, (tile, tile)))

    @pl.when(at == 0)
    def _():
        xb[...] = x[...].astype(jnp.bfloat16)

        def rows_of(b):
            after = columns(b) + 1.0
            for g in range(g_dev):
                def add(c, acc):
                    row = times[:, pl.ds(pl.multiple_of(c * tile, tile), tile)]
                    pick = (after == row).astype(jnp.bfloat16)
                    part = xb[HALO + g, pl.ds(pl.multiple_of(c * tile, tile), tile), :]
                    return acc + jnp.dot(pick, part, preferred_element_type=jnp.float32)

                acc = jnp.zeros((tile, cells), jnp.float32)
                acc = add(0, acc) if turns == 1 else lax.fori_loop(0, turns, add, acc)
                goal[g, pl.ds(pl.multiple_of(b * tile, tile), tile), :] = acc

        if turns == 1:
            rows_of(0)
        else:
            pl.loop(0, turns)(rows_of)

    for p in range(per):
        g = at * per + p
        for k in range(depth // cells):
            local = lax.rem(nb[g, k] - (me * g_dev + g) + HALO + width, width) + g
            inputs[p, :, k * cells : (k + 1) * cells] = xb[local]
        w = weights[p]

        def forward(b, matrix):
            part = pl.ds(pl.multiple_of(b * tile, tile), tile)
            out = lax.dot_general(
                inputs[p, part, :], matrix, (((1,), (1,)), ((), ())),
                preferred_element_type=jnp.float32,
            )
            live = (columns(b) != float(total - 1)).astype(jnp.float32)
            return (out * scale - goal[g, part, :]) * live

        def add_grad(b, acc):
            part = pl.ds(pl.multiple_of(b * tile, tile), tile)
            resid = forward(b, w).astype(jnp.bfloat16)
            return acc + lax.dot_general(
                resid, inputs[p, part, :], (((0,), (0,)), ((), ())),
                preferred_element_type=jnp.float32,
            )

        acc = jnp.zeros((cells, depth), jnp.float32)
        acc = add_grad(0, acc) if turns == 1 else lax.fori_loop(0, turns, add_grad, acc)
        fresh = w.astype(jnp.float32) - acc * (step_rate * 2.0 * scale / (total - 1))
        fresh_out[p] = fresh
        fresh_b = fresh.astype(jnp.bfloat16)

        def add_error(b, acc):
            out = forward(b, fresh_b)
            return acc + jnp.sum(out * out, axis=0, keepdims=True)

        acc = jnp.zeros((1, cells), jnp.float32)
        acc = add_error(0, acc) if turns == 1 else lax.fori_loop(0, turns, add_error, acc)
        error_out[pl.ds(g, 1), :] = acc * (1.0 / (total - 1))


def shards(snapshots, weights, neighbours, time_of):
    n = lax.axis_size("space")
    g_dev, cells, depth = weights.shape
    total = time_of.shape[0]
    span = g_dev + 2 * HALO
    x = gathered(snapshots, n)
    times = time_of.astype(jnp.float32).reshape(1, total)
    per = 2
    flops = 6 * g_dev * total * cells * depth
    return pl.pallas_call(
        functools.partial(step_kernel, n, per),
        grid=(g_dev // per,),
        out_shape=(
            jax.ShapeDtypeStruct(weights.shape, jnp.float32),
            jax.ShapeDtypeStruct((g_dev, cells), jnp.float32),
        ),
        in_specs=[
            pl.BlockSpec(memory_space=pltpu.SMEM),
            pl.BlockSpec((span, total, cells), lambda i: (0, 0, 0)),
            pl.BlockSpec((1, total), lambda i: (0, 0)),
            pl.BlockSpec((per, cells, depth), lambda i: (i, 0, 0)),
        ],
        out_specs=(
            pl.BlockSpec((per, cells, depth), lambda i: (i, 0, 0)),
            pl.BlockSpec((g_dev, cells), lambda i: (0, 0)),
        ),
        scratch_shapes=[
            pltpu.VMEM((g_dev, total, cells), jnp.float32),
            pltpu.VMEM((per, total, depth), jnp.bfloat16),
            pltpu.VMEM((span, total, cells), jnp.bfloat16),
        ],
        compiler_params=pltpu.CompilerParams(vmem_limit_bytes=44 * 2**20),
        cost_estimate=pl.CostEstimate(
            flops=flops, bytes_accessed=6 * g_dev * cells * depth, transcendentals=0
        ),
    )(neighbours, x, times, weights)


def solution(mesh):
    return jax.shard_map(
        shards,
        mesh=mesh,
        in_specs=(
            P(("groups", "space"), None, None),
            P(("groups", "space"), None, None),
            P(("groups", "space"), None),
            P("groups"),
        ),
        out_specs=(P(("groups", "space"), None, None), P(("groups", "space"), None)),
        check_vma=False,
    )
```

time: 38.7 us -> 28.6 us (0.74)
  Pallas kernels: 0 us -> 23.9 us
  starting transfers between devices: 11.9 us -> 0 us
  waiting for transfers between devices: 8.62 us -> 0 us
  matrix products: 8.4 us -> 0 us
  other arithmetic: 4.87 us -> 0.66 us
  local copies, waits for them, and re-layouts: 3.91 us -> 3.22 us
    pallas_call x0 -> x2, Pallas kernels: none -> 23.9 us  [the longest x1 17.7 us: gathered(): pl.pallas_call(functools.partial(gather_kernel, n), out_shape=jax.ShapeDt...]
    dot_general x2 -> x0, matrix products: 8.4 us -> none  [the longest x1 5.49 us: add_grad(): jnp.einsum('tgo,tgc->goc', resid, inputs, preferred_element_type=jnp.floa...]
    all_to_all x1 -> x0, starting transfers between devices: 7.39 us -> none  [shards(): lax.all_to_all(snapshots, 'space', split_axis=1, concat_axis=0, tiled=True)]
    all_to_all x1 -> x0, waiting for transfers between devices: 6.06 us -> none  [shards(): lax.all_to_all(snapshots, 'space', split_axis=1, concat_axis=0, tiled=True)]
    ppermute x2 -> x0, starting transfers between devices: 4.49 us -> none  [the longest x1 4.43 us: extended(): after = lax.ppermute(initial, axis, down)]
    sort x1 -> x0, other arithmetic: 3.19 us -> none  [shards(): order = jnp.argsort(time_of)]
    ppermute x2 -> x0, waiting for transfers between devices: 2.56 us -> none  [the longest x1 2.55 us: extended(): before = lax.ppermute(last, axis, up)]
    gather x3 -> x0, local copies, waits for them, and re-layouts: 1.79 us -> none  [the longest x1 0.95 us: block_rows(): inputs = rows[:, local].reshape(rows_step, g_dev, span)]
  transfers between devices with their start and end apart: 3 -> 0, of which waited for: 2 -> 0; matrix products, arithmetic and copies ran while one was open for 11% -> 0% of each run, Pallas kernels for 0% -> 0%
where the time goes in v1:
time: 28.6 us; the launch traced here: 28.4 us
  Pallas kernels  23.9 us (84%)
  local copies, waits for them, and re-layouts  3.22 us (11%)
  other arithmetic  0.66 us (2%)
  between operations  0.65 us (2%)
    pallas_call x1, Pallas kernels, gathered(): pl.pallas_call(functools.partial(gather_kernel, n), out_shape=jax.ShapeDt...  17.7 us
    pallas_call x1, Pallas kernels, shards(): pl.pallas_call(functools.partial(step_kernel, n, per), grid=(g_dev // per...  6.21 us
    unnamed x6, local copies, waits for them, and re-layouts  3.22 us
    reshape x1, other arithmetic, shards(): times = time_of.astype(jnp.float32).reshape(1, total)  0.66 us

profile of v1, /device:TPU:0, one launch (start us, length us, event | category | flops | bytes accessed | tf_op | source)
XLA Modules:
  0.0 28.4 jit_solution(3254119160518989231)
XLA Ops:
  0.6 0.7 %convert_bitcast_fusion.times = f32[1,128]{1,0:T(1,128)S(1)} fusion(s32[128]{0:T(128)} %param.7), kind=kLoop, calls=%fused_computation | loop fusion | flops 128 | bytes 1024 | tf_op jit(solution)/shard_map/reshape | solution.py:184
  1.3 0.0 copy-start.1
  1.3 0.9 %copy-done.1 = bf16[8,128,128]{2,1,0:T(8,128)(2,1)S(1)} copy-done((bf16[8,128,128]{2,1,0:T(8,128)(2,1)S(1)}, bf16[8,128,128]{2,1,0:T(8,128)(2,1)}, u32[]{:S(2)}) %copy-start.1) | copy-done | bytes 262168
  2.2 17.7 %shard_map.59.x = f32[16,128,128]{2,1,0:T(8,128)S(1)} custom-call(bf16[8,128,128]{2,1,0:T(8,128)(2,1)S(1)} %copy-done.1), custom_call_target="tpu_custom_call" | custom-call | bytes 1048576 | tf_op jit(solution)/shard_map/pallas_call | solution.py:80
  19.9 0.0 copy-start
  19.9 1.6 %copy-done = bf16[8,128,1024]{2,1,0:T(8,128)(2,1)S(1)} copy-done((bf16[8,128,1024]{2,1,0:T(8,128)(2,1)S(1)}, bf16[8,128,1024]{2,1,0:T(8,128)(2,1)}, u32[]{:S(2)}) %copy-start) | copy-done | bytes 2097176
  21.5 0.0 copy-start.2
  21.5 0.7 %copy-done.2 = s32[8,8]{1,0:T(8,128)S(1)} copy-done((s32[8,8]{1,0:T(8,128)S(1)}, s32[8,8]{1,0:T(8,128)}, u32[]{:S(2)}) %copy-start.2) | copy-done | bytes 280
  22.2 6.2 %shard_map.60 = (f32[8,128,1024]{2,1,0:T(8,128)}, f32[8,128]{1,0:T(8,128)}) custom-call(s32[8,8]{1,0:T(8,128)S(1)} %copy-done.2, f32[16,128,128]{2,1,0:T(8,128)S(1)} %shard_map.59.x, f32[1,128]{1,0:T(1,128)S(1)} %convert_bitcast_fusion.times, bf16[8,128,1024]{2,1,0:T(8,128)(2,1)S(1)} %copy-done), custom_call_target="tpu_custom_call" | custom-call | flops 805306368 | bytes 6291456 | tf_op jit(solution)/shard_map/pallas_call | solution.py:187
Async XLA Ops:
  1.3 0.9 %copy-start.1 = (bf16[8,128,128]{2,1,0:T(8,128)(2,1)S(1)}, bf16[8,128,128]{2,1,0:T(8,128)(2,1)}, u32[]{:S(2)}) copy-start(bf16[8,128,128]{2,1,0:T(8,128)(2,1)} %snaps.1) | copy-start | bytes 786436
  19.9 1.6 %copy-start = (bf16[8,128,1024]{2,1,0:T(8,128)(2,1)S(1)}, bf16[8,128,1024]{2,1,0:T(8,128)(2,1)}, u32[]{:S(2)}) copy-start(bf16[8,128,1024]{2,1,0:T(8,128)(2,1)} %weights.1) | copy-start | bytes 6291460
  21.5 0.7 %copy-start.2 = (s32[8,8]{1,0:T(8,128)S(1)}, s32[8,8]{1,0:T(8,128)}, u32[]{:S(2)}) copy-start(s32[8,8]{1,0:T(8,128)} %nb.1) | copy-start | bytes 772

commit v2 on v1

v2 whole, which is shorter than its diff:
```python
import functools

import jax
import jax.numpy as jnp
from jax import lax
from jax.experimental import pallas as pl
from jax.experimental.pallas import tpu as pltpu
from jax.sharding import PartitionSpec as P

HALO = 4
LIMIT = 50 * 2**20
MESH = pl.DeviceIdType.MESH


def partner(q, i, count):
    if count & (count - 1):
        return lax.rem(q + i, count), lax.rem(q + count - i, count)
    bit = 1
    out = q
    while bit <= i:
        if i & bit:
            out = out + bit * (1 - 2 * lax.rem(q // bit, 2))
        bit *= 2
    return out, out


def gather_kernel(n, snaps_hbm, w_hbm, nb_hbm, times_hbm, x, w, nb, times, snaps, wide, flat, pairs, siblings, load_sem, sems):
    rows, groups, cells = snaps.shape
    g_dev = groups // n
    span = g_dev + 2 * HALO
    chips = n // 2
    own_part = g_dev * rows
    me = lax.axis_index("space")
    q, core = me // 2, lax.rem(me, 2)
    other = 1 - core
    sibling = 2 * q + other

    load = pltpu.make_async_copy(snaps_hbm, snaps, load_sem.at[0])
    load.start()
    others = [
        pltpu.make_async_copy(a, b, load_sem.at[1 + i])
        for i, (a, b) in enumerate([(w_hbm, w), (nb_hbm, nb), (times_hbm, times)])
    ]
    barrier = pltpu.get_barrier_semaphore()
    for to in [2 * partner(q, i, chips)[0] + core for i in range(1, chips)] + [sibling]:
        pl.semaphore_signal(barrier, inc=1, device_id={"space": to}, device_id_type=MESH)
    load.wait()

    step = 16

    def relay(b):
        first = b * step
        block = snaps[:, pl.ds(first, step), :].astype(jnp.float32)
        wide[b % 2] = block.reshape(rows * step, cells)
        for p in range(step // 2):
            pair = jnp.concatenate(
                [wide[b % 2, pl.ds(2 * p + h, rows, stride=step), :] for h in range(2)], axis=0
            )
            at = (first + HALO + 2 * p) * rows
            flat[at : at + 2 * rows, :] = pair.astype(jnp.bfloat16)

    for b in range(groups // step):
        relay(b)

    edge = HALO * rows
    flat[:edge, :] = flat[groups * rows : groups * rows + edge, :]
    flat[(groups + HALO) * rows :, :] = flat[edge : 2 * edge, :]

    pl.semaphore_wait(barrier, chips)

    def chip_part(chip, length, skip=0):
        at = pl.multiple_of(chip * (2 * own_part) + skip * own_part, own_part)
        return flat.at[pl.ds(at, length * rows), :]

    def across(i):
        to = partner(q, i, chips)[0]
        return pltpu.make_async_remote_copy(
            src_ref=chip_part(to, span + g_dev),
            dst_ref=pairs.at[q],
            send_sem=sems.at[0, i],
            recv_sem=sems.at[1, i],
            device_id={"space": 2 * to + core},
            device_id_type=MESH,
        )

    def beside(i):
        source = partner(q, i, chips)[1]
        at = pl.ds(pl.multiple_of(other * own_part, own_part), span * rows)
        return pltpu.make_async_remote_copy(
            src_ref=chip_part(q, span, other) if i == 0 else pairs.at[source, at, :],
            dst_ref=siblings.at[source],
            send_sem=sems.at[2, i],
            recv_sem=sems.at[3, i],
            device_id={"space": sibling},
            device_id_type=MESH,
        )

    def place(device, block):
        at = pl.multiple_of(device * rows, rows)
        x[:, pl.ds(at, rows), :] = block.astype(jnp.float32).reshape(span, rows, cells)

    send_order = send_order_of(chips)
    wait_order = wait_order_of(chips)
    for i in send_order:
        across(i).start()
    beside(0).start()
    for other_load in others:
        other_load.start()
    place(me, chip_part(q, span, core)[...])
    for i in wait_order:
        across(i).wait_recv()
        beside(i).start()
        source = partner(q, i, chips)[1]
        at = pl.ds(pl.multiple_of(core * own_part, own_part), span * rows)
        place(2 * source + core, pairs[source, at, :])
    for i in [0] + wait_order:
        beside(i).wait_recv()
        source = partner(q, i, chips)[1] if i else q
        place(2 * source + other, siblings[source])
    for i in [0] + wait_order:
        beside(i).wait_send()
        if i:
            across(i).wait_send()
    for other_load in others:
        other_load.wait()


def send_order_of(chips):
    return list(range(chips - 1, 0, -1))


def wait_order_of(chips):
    return list(range(1, chips // 2)) + list(range(chips - 1, chips // 2 - 1, -1))


def gathered(snaps, weights, neighbours, times, n):
    rows, groups, cells = snaps.shape
    g_dev = groups // n
    span = g_dev + 2 * HALO
    chips = n // 2
    block = rows * cells
    need = (
        2 * groups * block
        + 2 * 16 * block * 4
        + 2 * (groups + 2 * HALO) * block
        + 2 * chips * (2 * span + g_dev) * block
        + 4 * span * n * block
    )
    return pl.pallas_call(
        functools.partial(gather_kernel, n),
        out_shape=[
            jax.ShapeDtypeStruct((span, rows * n, cells), jnp.float32),
            jax.ShapeDtypeStruct(weights.shape, weights.dtype),
            jax.ShapeDtypeStruct(neighbours.shape, neighbours.dtype),
            jax.ShapeDtypeStruct(times.shape, times.dtype),
        ],
        in_specs=[pl.BlockSpec(memory_space=pltpu.HBM)] * 4,
        out_specs=[pl.BlockSpec(memory_space=pltpu.VMEM)] * 4,
        scratch_shapes=[
            pltpu.VMEM(snaps.shape, jnp.bfloat16),
            pltpu.VMEM((2, rows * 16, cells), jnp.float32),
            pltpu.VMEM(((groups + 2 * HALO) * rows, cells), jnp.bfloat16),
            pltpu.VMEM((chips, (span + g_dev) * rows, cells), jnp.bfloat16),
            pltpu.VMEM((chips, span * rows, cells), jnp.bfloat16),
            pltpu.SemaphoreType.DMA((4,)),
            pltpu.SemaphoreType.DMA((4, chips)),
        ],
        compiler_params=pltpu.CompilerParams(
            collective_id=0, has_side_effects=True, vmem_limit_bytes=LIMIT
        ),
        cost_estimate=pl.CostEstimate(
            flops=0, bytes_accessed=4 * span * rows * n * cells * 20, transcendentals=0
        ),
    )(snaps, weights, neighbours, times)


def step_kernel(n, nb, x, times_in, weights, fresh_hbm, error_out, times, live, goal, inputs, xb, fresh_all, sems):
    span, total, cells = x.shape
    g_dev = span - 2 * HALO
    width = g_dev * n
    depth = weights.shape[2]
    scale = 1.0 / (depth**0.5)
    step_rate = 100.0
    me = lax.axis_index("space")
    tile = 128
    turns = total // tile

    def each(body, init):
        return body(0, init) if turns == 1 else lax.fori_loop(0, turns, body, init)

    def part_of(b):
        return pl.ds(b * tile if isinstance(b, int) else pl.multiple_of(b * tile, tile), tile)

    times[...] = times_in[...].astype(jnp.float32)
    xb[...] = x[...].astype(jnp.bfloat16)

    def rows_of(b, none):
        own = jnp.transpose(jnp.broadcast_to(times[:, part_of(b)], (tile, tile)))
        live[part_of(b), :] = (own != float(total - 1)).astype(jnp.float32)
        for g in range(0, g_dev, 2):
            def add(c, acc):
                pick = (own + 1.0 == times[:, part_of(c)]).astype(jnp.bfloat16)
                block = jnp.concatenate(
                    [xb[HALO + g + h, part_of(c), :] for h in range(2)], axis=1
                )
                return acc + jnp.dot(pick, block, preferred_element_type=jnp.float32)

            acc = each(add, jnp.zeros((tile, 2 * cells), jnp.float32))
            for h in range(2):
                goal[g + h, part_of(b), :] = acc[:, h * cells : (h + 1) * cells]
        return none

    each(rows_of, 0)

    copies = []
    for g in range(g_dev):
        for k in range(depth // cells):
            local = lax.rem(nb[g, k] - (me * g_dev + g) + HALO + width, width) + g
            inputs[g, :, k * cells : (k + 1) * cells] = xb[local]
        w = weights[g]

        def forward(b, matrix):
            out = lax.dot_general(
                inputs[g, part_of(b), :], matrix, (((1,), (1,)), ((), ())),
                preferred_element_type=jnp.float32,
            )
            return (out * scale - goal[g, part_of(b), :]) * live[part_of(b), :]

        def add_grad(b, acc):
            resid = forward(b, w).astype(jnp.bfloat16)
            return acc + lax.dot_general(
                resid, inputs[g, part_of(b), :], (((0,), (0,)), ((), ())),
                preferred_element_type=jnp.float32,
            )

        grad = each(add_grad, jnp.zeros((cells, depth), jnp.float32))
        fresh = w.astype(jnp.float32) - grad * (step_rate * 2.0 * scale / (total - 1))
        fresh_all[g] = fresh
        copies.append(pltpu.make_async_copy(fresh_all.at[g], fresh_hbm.at[g], sems.at[g]))
        copies[-1].start()
        fresh_b = fresh.astype(jnp.bfloat16)

        def add_error(b, acc):
            out = forward(b, fresh_b)
            return acc + jnp.sum(out * out, axis=0, keepdims=True)

        error = each(add_error, jnp.zeros((1, cells), jnp.float32))
        error_out[g : g + 1, :] = error * (1.0 / (total - 1))
    for copy in copies:
        copy.wait()


def shards(snapshots, weights, neighbours, time_of):
    n = lax.axis_size("space")
    g_dev, cells, depth = weights.shape
    total = time_of.shape[0]
    span = g_dev + 2 * HALO
    x, weights, neighbours, times = gathered(
        snapshots, weights, neighbours, time_of.reshape(1, total), n
    )
    flops = 6 * g_dev * total * cells * depth
    words = g_dev * cells * depth
    need = (
        6 * words
        + 2 * span * total * cells
        + 4 * (g_dev + 1) * total * cells
        + 2 * g_dev * total * depth
        + 4 * span * total * cells
    )
    return pl.pallas_call(
        functools.partial(step_kernel, n),
        out_shape=(
            jax.ShapeDtypeStruct(weights.shape, jnp.float32),
            jax.ShapeDtypeStruct((g_dev, cells), jnp.float32),
        ),
        in_specs=[
            pl.BlockSpec(memory_space=pltpu.SMEM),
            pl.BlockSpec(memory_space=pltpu.VMEM),
            pl.BlockSpec(memory_space=pltpu.VMEM),
            pl.BlockSpec(memory_space=pltpu.VMEM),
        ],
        out_specs=(
            pl.BlockSpec(memory_space=pltpu.HBM),
            pl.BlockSpec(memory_space=pltpu.VMEM),
        ),
        scratch_shapes=[
            pltpu.VMEM((1, total), jnp.float32),
            pltpu.VMEM((total, cells), jnp.float32),
            pltpu.VMEM((g_dev, total, cells), jnp.float32),
            pltpu.VMEM((g_dev, total, depth), jnp.bfloat16),
            pltpu.VMEM((span, total, cells), jnp.bfloat16),
            pltpu.VMEM((g_dev, cells, depth), jnp.float32),
            pltpu.SemaphoreType.DMA((g_dev,)),
        ],
        compiler_params=pltpu.CompilerParams(vmem_limit_bytes=need + 4 * 2**20),
        cost_estimate=pl.CostEstimate(
            flops=flops, bytes_accessed=3 * words, transcendentals=0
        ),
    )(neighbours, x, times, weights)


def solution(mesh):
    return jax.shard_map(
        shards,
        mesh=mesh,
        in_specs=(
            P(("groups", "space"), None, None),
            P(("groups", "space"), None, None),
            P(("groups", "space"), None),
            P("groups"),
        ),
        out_specs=(P(("groups", "space"), None, None), P(("groups", "space"), None)),
        check_vma=False,
    )
```

time: 28.6 us -> 25.3 us (0.88)
  Pallas kernels: 23.9 us -> 22.2 us
  local copies, waits for them, and re-layouts: 3.22 us -> 2.28 us
  other arithmetic: 0.66 us -> 0 us
    pallas_call x2, Pallas kernels: 23.9 us -> 22.2 us  [the longest x1 16.6 us: gathered(): pl.pallas_call(functools.partial(gather_kernel, n), out_shape=[jax.ShapeD...]
    unnamed x6, local copies, waits for them, and re-layouts: 3.22 us -> 2.28 us
    reshape x1 -> x0, other arithmetic: 0.66 us -> none  [shards(): times = time_of.astype(jnp.float32).reshape(1, total)]
where the time goes in v2:
time: 25.3 us; the launch traced here: 25.1 us
  Pallas kernels  22.2 us (88%)
  local copies, waits for them, and re-layouts  2.28 us (9%)
  between operations  0.65 us (3%)
    pallas_call x1, Pallas kernels, gathered(): pl.pallas_call(functools.partial(gather_kernel, n), out_shape=[jax.ShapeD...  16.6 us
    pallas_call x1, Pallas kernels, shards(): pl.pallas_call(functools.partial(step_kernel, n), out_shape=(jax.ShapeDty...  5.56 us
    unnamed x6, local copies, waits for them, and re-layouts  2.28 us

profile of v2, /device:TPU:0, one launch (start us, length us, event | category | flops | bytes accessed | tf_op | source)
XLA Modules:
  0.0 25.1 jit_solution(14758884241237447395)
XLA Ops:
  0.6 0.0 copy-start
  0.6 0.9 %copy-done = bf16[8,128,128]{2,1,0:T(8,128)(2,1)S(1)} copy-done((bf16[8,128,128]{2,1,0:T(8,128)(2,1)S(1)}, bf16[8,128,128]{2,1,0:T(8,128)(2,1)}, u32[]{:S(2)}) %copy-start) | copy-done | bytes 262168
  1.6 0.0 copy-start.1
  1.6 0.7 %copy-done.1 = s32[8,8]{1,0:T(8,128)S(1)} copy-done((s32[8,8]{1,0:T(8,128)S(1)}, s32[8,8]{1,0:T(8,128)}, u32[]{:S(2)}) %copy-start.1) | copy-done | bytes 280
  2.3 0.0 copy-start.2
  2.3 0.7 %copy-done.2 = s32[128]{0:T(128)S(1)} copy-done((s32[128]{0:T(128)S(1)}, s32[128]{0:T(128)}, u32[]{:S(2)}) %copy-start.2) | copy-done | bytes 536
  2.9 16.6 %shard_map.59 = (f32[16,128,128]{2,1,0:T(8,128)S(1)}, bf16[8,128,1024]{2,1,0:T(8,128)(2,1)S(1)}, s32[8,8]{1,0:T(8,128)S(1)}, s32[1,128]{1,0:T(1,128)S(1)}) custom-call(bf16[8,128,128]{2,1,0:T(8,128)(2,1)S(1)} %copy-done, bf16[8,128,1024]{2,1,0:T(8,128)(2,1)} %w_hbm.1, s32[8,8]{1,0:T(8,128)S(1)} %copy-done.1, s32[1,128]{1,0:T(1,128)S(1)} %bitcast.1), custom_call_target="tpu_custom_call" | custom-call | bytes 20971520 | tf_op jit(solution)/shard_map/pallas_call | solution.py:149
  19.6 5.6 %shard_map.60 = (f32[8,128,1024]{2,1,0:T(8,128)}, f32[8,128]{1,0:T(8,128)}) custom-call(s32[8,8]{1,0:T(8,128)S(1)} %get-tuple-element.6.nb, f32[16,128,128]{2,1,0:T(8,128)S(1)} %get-tuple-element.7.x, s32[1,128]{1,0:T(1,128)S(1)} %get-tuple-element.8.times_in, bf16[8,128,1024]{2,1,0:T(8,128)(2,1)S(1)} %get-tuple-element.9.weights), custom_call_target="tpu_custom_call" | custom-call | flops 805306368 | bytes 3145728 | tf_op jit(solution)/shard_map/pallas_call | solution.py:270
Async XLA Ops:
  0.6 1.0 %copy-start = (bf16[8,128,128]{2,1,0:T(8,128)(2,1)S(1)}, bf16[8,128,128]{2,1,0:T(8,128)(2,1)}, u32[]{:S(2)}) copy-start(bf16[8,128,128]{2,1,0:T(8,128)(2,1)} %snaps_hbm.1) | copy-start | bytes 786436
  1.6 0.7 %copy-start.1 = (s32[8,8]{1,0:T(8,128)S(1)}, s32[8,8]{1,0:T(8,128)}, u32[]{:S(2)}) copy-start(s32[8,8]{1,0:T(8,128)} %nb_hbm.1) | copy-start | bytes 772
  2.3 0.7 %copy-start.2 = (s32[128]{0:T(128)S(1)}, s32[128]{0:T(128)}, u32[]{:S(2)}) copy-start(s32[128]{0:T(128)} %param.7) | copy-start | bytes 1540

commit v3 on v2

v3 whole, which is shorter than its diff:
```python
import functools

import jax
import jax.numpy as jnp
from jax import lax
from jax.experimental import pallas as pl
from jax.experimental.pallas import tpu as pltpu
from jax.sharding import PartitionSpec as P

HALO = 4
LIMIT = 58 * 2**20
MESH = pl.DeviceIdType.MESH


def partner(q, i, count):
    if count & (count - 1):
        return lax.rem(q + i, count), lax.rem(q + count - i, count)
    bit = 1
    out = q
    while bit <= i:
        if i & bit:
            out = out + bit * (1 - 2 * lax.rem(q // bit, 2))
        bit *= 2
    return out, out


def gather_kernel(n, snaps_hbm, x_hbm, snaps, wide, flat, pairs, siblings, x, xb, load_sem, sems):
    rows, groups, cells = snaps.shape
    g_dev = groups // n
    span = g_dev + 2 * HALO
    chips = n // 2
    own_part = g_dev * rows
    me = lax.axis_index("space")
    q, core = me // 2, lax.rem(me, 2)
    other = 1 - core
    sibling = 2 * q + other

    load = pltpu.make_async_copy(snaps_hbm, snaps, load_sem.at[0])
    load.start()
    barrier = pltpu.get_barrier_semaphore()
    for to in [2 * partner(q, i, chips)[0] + core for i in range(1, chips)] + [sibling]:
        pl.semaphore_signal(barrier, inc=1, device_id={"space": to}, device_id_type=MESH)
    load.wait()

    step = 16

    def relay(b):
        first = b * step
        block = snaps[:, pl.ds(first, step), :].astype(jnp.float32)
        wide[b % 2] = block.reshape(rows * step, cells)
        for p in range(step // 2):
            pair = jnp.concatenate(
                [wide[b % 2, pl.ds(2 * p + h, rows, stride=step), :] for h in range(2)], axis=0
            )
            at = (first + HALO + 2 * p) * rows
            flat[at : at + 2 * rows, :] = pair.astype(jnp.bfloat16)

    for b in range(groups // step):
        relay(b)

    edge = HALO * rows
    flat[:edge, :] = flat[groups * rows : groups * rows + edge, :]
    flat[(groups + HALO) * rows :, :] = flat[edge : 2 * edge, :]

    pl.semaphore_wait(barrier, chips)

    def chip_part(chip, length, skip=0):
        at = pl.multiple_of(chip * (2 * own_part) + skip * own_part, own_part)
        return flat.at[pl.ds(at, length * rows), :]

    def across(i):
        to = partner(q, i, chips)[0]
        return pltpu.make_async_remote_copy(
            src_ref=chip_part(to, span + g_dev),
            dst_ref=pairs.at[q],
            send_sem=sems.at[0, i],
            recv_sem=sems.at[1, i],
            device_id={"space": 2 * to + core},
            device_id_type=MESH,
        )

    def beside(i):
        source = partner(q, i, chips)[1]
        at = pl.ds(pl.multiple_of(other * own_part, own_part), span * rows)
        return pltpu.make_async_remote_copy(
            src_ref=chip_part(q, span, other) if i == 0 else pairs.at[source, at, :],
            dst_ref=siblings.at[source],
            send_sem=sems.at[2, i],
            recv_sem=sems.at[3, i],
            device_id={"space": sibling},
            device_id_type=MESH,
        )

    def place(device, block):
        at = pl.multiple_of(device * rows, rows)
        x[:, pl.ds(at, rows), :] = block.astype(jnp.float32).reshape(span, rows, cells)

    send_order = send_order_of(chips)
    wait_order = wait_order_of(chips)
    for i in send_order:
        across(i).start()
    beside(0).start()
    place(me, chip_part(q, span, core)[...])
    for i in wait_order:
        across(i).wait_recv()
        beside(i).start()
        source = partner(q, i, chips)[1]
        at = pl.ds(pl.multiple_of(core * own_part, own_part), span * rows)
        place(2 * source + core, pairs[source, at, :])
    for i in [0] + wait_order:
        beside(i).wait_recv()
        source = partner(q, i, chips)[1] if i else q
        place(2 * source + other, siblings[source])
    stores = []
    for s in range(4):
        part = pl.ds(s * span // 4, span // 4)
        xb[part] = x[part].astype(jnp.bfloat16)
        stores.append(
            pltpu.make_async_copy(xb.at[part], x_hbm.at[part], load_sem.at[1 + s])
        )
        stores[-1].start()
    for i in [0] + wait_order:
        beside(i).wait_send()
        if i:
            across(i).wait_send()
    for store in stores:
        store.wait()


def send_order_of(chips):
    return list(range(chips - 1, 0, -1))


def wait_order_of(chips):
    return list(range(1, chips // 2)) + list(range(chips - 1, chips // 2 - 1, -1))


def gathered(snaps, n):
    rows, groups, cells = snaps.shape
    g_dev = groups // n
    span = g_dev + 2 * HALO
    chips = n // 2
    return pl.pallas_call(
        functools.partial(gather_kernel, n),
        out_shape=jax.ShapeDtypeStruct((span, rows * n, cells), jnp.bfloat16),
        in_specs=[pl.BlockSpec(memory_space=pltpu.HBM)],
        out_specs=pl.BlockSpec(memory_space=pltpu.HBM),
        scratch_shapes=[
            pltpu.VMEM(snaps.shape, jnp.bfloat16),
            pltpu.VMEM((2, rows * 16, cells), jnp.float32),
            pltpu.VMEM(((groups + 2 * HALO) * rows, cells), jnp.bfloat16),
            pltpu.VMEM((chips, (span + g_dev) * rows, cells), jnp.bfloat16),
            pltpu.VMEM((chips, span * rows, cells), jnp.bfloat16),
            pltpu.VMEM((span, rows * n, cells), jnp.float32),
            pltpu.VMEM((span, rows * n, cells), jnp.bfloat16),
            pltpu.SemaphoreType.DMA((5,)),
            pltpu.SemaphoreType.DMA((4, chips)),
        ],
        compiler_params=pltpu.CompilerParams(
            collective_id=0, has_side_effects=True, vmem_limit_bytes=LIMIT
        ),
        cost_estimate=pl.CostEstimate(
            flops=0, bytes_accessed=4 * span * rows * n * cells, transcendentals=0
        ),
    )(snaps)


def step_kernel(n, nb_hbm, x_hbm, times_hbm, w_hbm, fresh_hbm, error_out, nb, xb, times_in, weights, times, live, goal, inputs, resids, rounded, fresh_all, load_sem, sems):
    span, total, cells = xb.shape
    g_dev = span - 2 * HALO
    width = g_dev * n
    depth = weights.shape[2]
    scale = 1.0 / (depth**0.5)
    step_rate = 100.0
    me = lax.axis_index("space")
    tile = 128
    turns = total // tile

    loads = [
        pltpu.make_async_copy(a, b, load_sem.at[i])
        for i, (a, b) in enumerate(
            [(times_hbm, times_in), (x_hbm, xb), (nb_hbm, nb), (w_hbm, weights)]
        )
    ]
    for load in loads:
        load.start()

    def each(body, init):
        return body(0, init) if turns == 1 else lax.fori_loop(0, turns, body, init)

    def part_of(b):
        return pl.ds(b * tile if isinstance(b, int) else pl.multiple_of(b * tile, tile), tile)

    loads[0].wait()
    times[...] = times_in[...].astype(jnp.float32)
    loads[1].wait()

    def rows_of(b, none):
        own = jnp.transpose(jnp.broadcast_to(times[:, part_of(b)], (tile, tile)))
        live[part_of(b), :] = (own != float(total - 1)).astype(jnp.float32)
        for g in range(0, g_dev, 2):
            def add(c, acc):
                pick = (own + 1.0 == times[:, part_of(c)]).astype(jnp.bfloat16)
                block = jnp.concatenate(
                    [xb[HALO + g + h, part_of(c), :] for h in range(2)], axis=1
                )
                return acc + jnp.dot(pick, block, preferred_element_type=jnp.float32)

            acc = each(add, jnp.zeros((tile, 2 * cells), jnp.float32))
            for h in range(2):
                goal[g + h, part_of(b), :] = acc[:, h * cells : (h + 1) * cells]
        return none

    each(rows_of, 0)
    for load in loads[2:]:
        load.wait()

    def forward(g, b, matrix):
        out = lax.dot_general(
            inputs[g, part_of(b), :], matrix, (((1,), (1,)), ((), ())),
            preferred_element_type=jnp.float32,
        )
        return (out * scale - goal[g, part_of(b), :]) * live[part_of(b), :]

    def predict(g):
        for k in range(depth // cells):
            local = lax.rem(nb[g, k] - (me * g_dev + g) + HALO + width, width) + g
            inputs[g, :, k * cells : (k + 1) * cells] = xb[local]

        def one(b, none):
            resids[g, part_of(b), :] = forward(g, b, weights[g]).astype(jnp.bfloat16)
            return none

        each(one, 0)

    def update(g):
        def add(b, acc):
            return acc + lax.dot_general(
                resids[g, part_of(b), :], inputs[g, part_of(b), :], (((0,), (0,)), ((), ())),
                preferred_element_type=jnp.float32,
            )

        grad = each(add, jnp.zeros((cells, depth), jnp.float32))
        fresh = weights[g].astype(jnp.float32) - grad * (
            step_rate * 2.0 * scale / (total - 1)
        )
        fresh_all[g] = fresh
        rounded[g] = fresh.astype(jnp.bfloat16)

    def judge(g):
        def add(b, acc):
            out = forward(g, b, rounded[g])
            return acc + jnp.sum(out * out, axis=0, keepdims=True)

        error = each(add, jnp.zeros((1, cells), jnp.float32))
        error_out[g : g + 1, :] = error * (1.0 / (total - 1))

    copies = []
    for g in range(g_dev + 2):
        if g < g_dev:
            predict(g)
        if 1 <= g <= g_dev:
            update(g - 1)
        if g >= 2:
            judge(g - 2)
        if g >= 2 and g % 2 == 0:
            part = pl.ds(g - 2, 2)
            copies.append(
                pltpu.make_async_copy(fresh_all.at[part], fresh_hbm.at[part], sems.at[g // 2 - 1])
            )
            copies[-1].start()
    for copy in copies:
        copy.wait()


def shards(snapshots, weights, neighbours, time_of):
    n = lax.axis_size("space")
    g_dev, cells, depth = weights.shape
    total = time_of.shape[0]
    span = g_dev + 2 * HALO
    x = gathered(snapshots, n)
    words = g_dev * cells * depth
    return pl.pallas_call(
        functools.partial(step_kernel, n),
        out_shape=(
            jax.ShapeDtypeStruct(weights.shape, jnp.float32),
            jax.ShapeDtypeStruct((g_dev, cells), jnp.float32),
        ),
        in_specs=[pl.BlockSpec(memory_space=pltpu.HBM)] * 4,
        out_specs=(
            pl.BlockSpec(memory_space=pltpu.HBM),
            pl.BlockSpec(memory_space=pltpu.VMEM),
        ),
        scratch_shapes=[
            pltpu.SMEM(neighbours.shape, jnp.int32),
            pltpu.VMEM(x.shape, jnp.bfloat16),
            pltpu.VMEM((1, total), jnp.int32),
            pltpu.VMEM(weights.shape, jnp.bfloat16),
            pltpu.VMEM((1, total), jnp.float32),
            pltpu.VMEM((total, cells), jnp.float32),
            pltpu.VMEM((g_dev, total, cells), jnp.float32),
            pltpu.VMEM((g_dev, total, depth), jnp.bfloat16),
            pltpu.VMEM((g_dev, total, cells), jnp.bfloat16),
            pltpu.VMEM(weights.shape, jnp.bfloat16),
            pltpu.VMEM(weights.shape, jnp.float32),
            pltpu.SemaphoreType.DMA((4,)),
            pltpu.SemaphoreType.DMA((g_dev // 2,)),
        ],
        compiler_params=pltpu.CompilerParams(vmem_limit_bytes=LIMIT),
        cost_estimate=pl.CostEstimate(
            flops=6 * total * words, bytes_accessed=6 * words, transcendentals=0
        ),
    )(neighbours, x, time_of.reshape(1, total), weights)


def solution(mesh):
    return jax.shard_map(
        shards,
        mesh=mesh,
        in_specs=(
            P(("groups", "space"), None, None),
            P(("groups", "space"), None, None),
            P(("groups", "space"), None),
            P("groups"),
        ),
        out_specs=(P(("groups", "space"), None, None), P(("groups", "space"), None)),
        check_vma=False,
    )
```

time: 25.3 us -> 23.9 us (0.945)
  local copies, waits for them, and re-layouts: 2.28 us -> 0 us
  Pallas kernels: 22.2 us -> 23.1 us
    unnamed x6 -> x0, local copies, waits for them, and re-layouts: 2.28 us -> none
    pallas_call x1, Pallas kernels: 16.6 us -> 17.3 us  [gathered(): pl.pallas_call(functools.partial(gather_kernel, n), out_shape=jax.ShapeDt...]
where the time goes in v3:
time: 23.9 us; the launch traced here: 23.7 us
  Pallas kernels  23.1 us (97%)
  between operations  0.64 us (3%)
    pallas_call x1, Pallas kernels, gathered(): pl.pallas_call(functools.partial(gather_kernel, n), out_shape=jax.ShapeDt...  17.3 us
    pallas_call x1, Pallas kernels, shards(): pl.pallas_call(functools.partial(step_kernel, n), out_shape=(jax.ShapeDty...  5.75 us

profile of v3, /device:TPU:0, one launch (start us, length us, event | category | flops | bytes accessed | tf_op | source)
XLA Modules:
  0.0 23.7 jit_solution(13566283024729163738)
XLA Ops:
  0.6 17.3 %shard_map.59.x_hbm = bf16[16,128,128]{2,1,0:T(8,128)(2,1)} custom-call(bf16[8,128,128]{2,1,0:T(8,128)(2,1)} %snaps_hbm.1), custom_call_target="tpu_custom_call" | custom-call | bytes 1048576 | tf_op jit(solution)/shard_map/pallas_call | solution.py:143
  17.9 5.8 %shard_map.60 = (f32[8,128,1024]{2,1,0:T(8,128)}, f32[8,128]{1,0:T(8,128)}) custom-call(s32[8,8]{1,0:T(8,128)} %nb_hbm.1, bf16[16,128,128]{2,1,0:T(8,128)(2,1)} %shard_map.59.x_hbm, s32[1,128]{1,0:T(1,128)} %bitcast.1, bf16[8,128,1024]{2,1,0:T(8,128)(2,1)} %w_hbm.1), custom_call_target="tpu_custom_call" | custom-call | flops 805306368 | bytes 6291456 | tf_op jit(solution)/shard_map/pallas_call | solution.py:283

commit v4 on v3

--- a/solution.py
+++ b/solution.py
@@ -24,7 +24,7 @@
     return out, out
 
 
-def gather_kernel(n, snaps_hbm, x_hbm, snaps, wide, flat, pairs, siblings, x, xb, load_sem, sems):
+def gather_kernel(n, snaps_hbm, x_hbm, snaps, wide, flat, pairs, siblings, x, xb, load_sem, store_sem, sems):
     rows, groups, cells = snaps.shape
     g_dev = groups // n
     span = g_dev + 2 * HALO
@@ -35,7 +35,7 @@
     other = 1 - core
     sibling = 2 * q + other
 
-    load = pltpu.make_async_copy(snaps_hbm, snaps, load_sem.at[0])
+    load = pltpu.make_async_copy(snaps_hbm, snaps, load_sem)
     load.start()
     barrier = pltpu.get_barrier_semaphore()
     for to in [2 * partner(q, i, chips)[0] + core for i in range(1, chips)] + [sibling]:
@@ -101,24 +101,29 @@
         across(i).start()
     beside(0).start()
     place(me, chip_part(q, span, core)[...])
-    for i in wait_order:
+    stores = []
+
+    def finish(i):
+        beside(i).wait_recv()
+        source = partner(q, i, chips)[1] if i else q
+        place(2 * source + other, siblings[source])
+        part = pl.ds(pl.multiple_of(source * 2 * rows, 2 * rows), 2 * rows)
+        xb[:, part, :] = x[:, part, :].astype(jnp.bfloat16)
+        stores.append(
+            pltpu.make_async_copy(xb.at[:, part, :], x_hbm.at[:, part, :], store_sem.at[i])
+        )
+        stores[-1].start()
+
+    for done, i in enumerate(wait_order):
         across(i).wait_recv()
         beside(i).start()
         source = partner(q, i, chips)[1]
         at = pl.ds(pl.multiple_of(core * own_part, own_part), span * rows)
         place(2 * source + core, pairs[source, at, :])
-    for i in [0] + wait_order:
-        beside(i).wait_recv()
-        source = partner(q, i, chips)[1] if i else q
-        place(2 * source + other, siblings[source])
-    stores = []
-    for s in range(4):
-        part = pl.ds(s * span // 4, span // 4)
-        xb[part] = x[part].astype(jnp.bfloat16)
-        stores.append(
-            pltpu.make_async_copy(xb.at[part], x_hbm.at[part], load_sem.at[1 + s])
-        )
-        stores[-1].start()
+        if done >= 2:
+            finish(([0] + wait_order)[done - 2])
+    for i in ([0] + wait_order)[max(chips - 3, 0):]:
+        finish(i)
     for i in [0] + wait_order:
         beside(i).wait_send()
         if i:
@@ -153,7 +158,8 @@
             pltpu.VMEM((chips, span * rows, cells), jnp.bfloat16),
             pltpu.VMEM((span, rows * n, cells), jnp.float32),
             pltpu.VMEM((span, rows * n, cells), jnp.bfloat16),
-            pltpu.SemaphoreType.DMA((5,)),
+            pltpu.SemaphoreType.DMA,
+            pltpu.SemaphoreType.DMA((chips,)),
             pltpu.SemaphoreType.DMA((4, chips)),
         ],
         compiler_params=pltpu.CompilerParams(
@@ -179,7 +185,8 @@
     loads = [
         pltpu.make_async_copy(a, b, load_sem.at[i])
         for i, (a, b) in enumerate(
-            [(times_hbm, times_in), (x_hbm, xb), (nb_hbm, nb), (w_hbm, weights)]
+            [(times_hbm, times_in), (x_hbm, xb), (nb_hbm, nb)]
+            + [(w_hbm.at[g], weights.at[g]) for g in range(g_dev)]
         )
     ]
     for load in loads:
@@ -212,8 +219,7 @@
         return none
 
     each(rows_of, 0)
-    for load in loads[2:]:
-        load.wait()
+    loads[2].wait()
 
     def forward(g, b, matrix):
         out = lax.dot_general(
@@ -256,19 +262,26 @@
         error_out[g : g + 1, :] = error * (1.0 / (total - 1))
 
     copies = []
+
+    def send(first, count):
+        part = pl.ds(first, count)
+        copies.append(
+            pltpu.make_async_copy(fresh_all.at[part], fresh_hbm.at[part], sems.at[first])
+        )
+        copies[-1].start()
+
     for g in range(g_dev + 2):
+        if g < g_dev and g % 4 == 0:
+            for load in loads[3 + g : 3 + g + 4]:
+                load.wait()
         if g < g_dev:
             predict(g)
         if 1 <= g <= g_dev:
             update(g - 1)
         if g >= 2:
             judge(g - 2)
-        if g >= 2 and g % 2 == 0:
-            part = pl.ds(g - 2, 2)
-            copies.append(
-                pltpu.make_async_copy(fresh_all.at[part], fresh_hbm.at[part], sems.at[g // 2 - 1])
-            )
-            copies[-1].start()
+        if 1 <= g <= g_dev and g % 2 == 0:
+            send(g - 2, 2)
     for copy in copies:
         copy.wait()
 
@@ -303,8 +316,8 @@
             pltpu.VMEM((g_dev, total, cells), jnp.bfloat16),
             pltpu.VMEM(weights.shape, jnp.bfloat16),
             pltpu.VMEM(weights.shape, jnp.float32),
-            pltpu.SemaphoreType.DMA((4,)),
-            pltpu.SemaphoreType.DMA((g_dev // 2,)),
+            pltpu.SemaphoreType.DMA((3 + g_dev,)),
+            pltpu.SemaphoreType.DMA((g_dev,)),
         ],
         compiler_params=pltpu.CompilerParams(vmem_limit_bytes=LIMIT),
         cost_estimate=pl.CostEstimate(

time: 23.9 us -> 23.6 us (0.987)
  Pallas kernels: 23.1 us -> 22.8 us
where the time goes in v4:
time: 23.6 us; the launch traced here: 23.4 us
  Pallas kernels  22.8 us (97%)
  between operations  0.64 us (3%)
    pallas_call x1, Pallas kernels, gathered(): pl.pallas_call(functools.partial(gather_kernel, n), out_shape=jax.ShapeDt...  17.2 us
    pallas_call x1, Pallas kernels, shards(): pl.pallas_call(functools.partial(step_kernel, n), out_shape=(jax.ShapeDty...  5.58 us

profile of v4, /device:TPU:0, one launch (start us, length us, event | category | flops | bytes accessed | tf_op | source)
XLA Modules:
  0.0 23.4 jit_solution(4497300873199877036)
XLA Ops:
  0.6 17.2 %shard_map.59.x_hbm = bf16[16,128,128]{2,1,0:T(8,128)(2,1)} custom-call(bf16[8,128,128]{2,1,0:T(8,128)(2,1)} %snaps_hbm.1), custom_call_target="tpu_custom_call" | custom-call | bytes 1048576 | tf_op jit(solution)/shard_map/pallas_call | solution.py:148
  17.9 5.6 %shard_map.60 = (f32[8,128,1024]{2,1,0:T(8,128)}, f32[8,128]{1,0:T(8,128)}) custom-call(s32[8,8]{1,0:T(8,128)} %nb_hbm.1, bf16[16,128,128]{2,1,0:T(8,128)(2,1)} %shard_map.59.x_hbm, s32[1,128]{1,0:T(1,128)} %bitcast.1, bf16[8,128,1024]{2,1,0:T(8,128)(2,1)} %w_hbm.1), custom_call_target="tpu_custom_call" | custom-call | flops 805306368 | bytes 6291456 | tf_op jit(solution)/shard_map/pallas_call | solution.py:296

commit v5 on v4

--- a/solution.py
+++ b/solution.py
@@ -114,15 +114,13 @@
         )
         stores[-1].start()
 
-    for done, i in enumerate(wait_order):
+    for i in wait_order:
         across(i).wait_recv()
         beside(i).start()
         source = partner(q, i, chips)[1]
         at = pl.ds(pl.multiple_of(core * own_part, own_part), span * rows)
         place(2 * source + core, pairs[source, at, :])
-        if done >= 2:
-            finish(([0] + wait_order)[done - 2])
-    for i in ([0] + wait_order)[max(chips - 3, 0):]:
+    for i in [0] + wait_order:
         finish(i)
     for i in [0] + wait_order:
         beside(i).wait_send()
@@ -133,7 +131,7 @@
 
 
 def send_order_of(chips):
-    return list(range(chips - 1, 0, -1))
+    return list(range(1, chips))
 
 
 def wait_order_of(chips):

time: 23.6 us -> 22.7 us (0.962)
  the two profiles are of different devices: /device:TPU:0 before, /device:TPU:1 now
where the time goes in v5:
time: 22.7 us; the launch traced here: 22.5 us
  Pallas kernels  21.9 us (96%)
  between operations  0.64 us (3%)
    pallas_call x1, Pallas kernels, gathered(): pl.pallas_call(functools.partial(gather_kernel, n), out_shape=jax.ShapeDt...  16.3 us
    pallas_call x1, Pallas kernels, shards(): pl.pallas_call(functools.partial(step_kernel, n), out_shape=(jax.ShapeDty...  5.6 us

profile of v5, /device:TPU:1, one launch (start us, length us, event | category | flops | bytes accessed | tf_op | source)
XLA Modules:
  0.0 22.5 jit_solution(3253612960829164412)
XLA Ops:
  0.6 16.3 %shard_map.59.x_hbm = bf16[16,128,128]{2,1,0:T(8,128)(2,1)} custom-call(bf16[8,128,128]{2,1,0:T(8,128)(2,1)} %snaps_hbm.1), custom_call_target="tpu_custom_call" | custom-call | bytes 1048576 | tf_op jit(solution)/shard_map/pallas_call | solution.py:146
  16.9 5.6 %shard_map.60 = (f32[8,128,1024]{2,1,0:T(8,128)}, f32[8,128]{1,0:T(8,128)}) custom-call(s32[8,8]{1,0:T(8,128)} %nb_hbm.1, bf16[16,128,128]{2,1,0:T(8,128)(2,1)} %shard_map.59.x_hbm, s32[1,128]{1,0:T(1,128)} %bitcast.1, bf16[8,128,1024]{2,1,0:T(8,128)(2,1)} %w_hbm.1), custom_call_target="tpu_custom_call" | custom-call | flops 805306368 | bytes 6291456 | tf_op jit(solution)/shard_map/pallas_call | solution.py:294
